TPU v7x, 512 devices: a whole 4x8x8 slice. The times are simulated.
512 devices in a mesh: batch: 32 (over z, x), blk: 16 (over y, core).
Axes of the slice: x: 4, y: 8, z: 8, core: 2. Of those that a mesh axis runs over, the one named last changes fastest.
Arguments:
- points: float32 [1024, 16, 3, 256], P('batch', 'blk'), may hold values from -6 to 6
- centers: float32 [1024, 16, 3, 384], P('batch', 'blk'), may hold values from -6 to 6
- exponents: float32 [1024, 16, 384], P('batch', 'blk'), may hold values from 0.1 to 1
- angular: float32 [1024, 16, 3, 384], P('batch', 'blk'), may hold values from -3 to 3
- grid_weights: float32 [1024, 16, 256], P('batch', 'blk'), may hold values from 0.001 to 0.01
- hartree: float32 [1024, 16, 256], P('batch', 'blk'), may hold values from 0 to 1.7
- load_plan: int32 [16, 1024], P('blk'), may hold values from 0 to 1023, each once within a row
- density_blocks: bfloat16 [256, 128, 128], P('blk'), may hold values from -0.046875 to 0.046875
- pair_lists: int32 [32, 16, 16, 2], P('batch', 'blk'), may hold values from 0 to 15
- batch_pairs: int32 [1024, 16, 9], P('batch', 'blk'), may hold values from 0 to 31, as said below
Outputs:
- hamiltonian: float32 [256, 128, 128], P('blk')
- density: float32 [1024, 16, 256], P('batch', 'blk')
Inputs may be any that keep to these rules, and one draw needn't show every extreme that they name: Each row of load_plan names every storage row of its column once. `pair_lists`: local index of a block pair within the 16 pairs held by one index of blk. `batch_pairs`: entry e of a device's table is the (e % 2)-th block it reads from index e // 2 of blk; every entry of a device's table is named by some pair of its batches.
All inputs are finite; a program needn't handle non-finite values.
Results may differ from a plain program's by a relative error of at most 0.0065.
Values may be sent and summed in bfloat16 or wider, within the bound.
No kernel may reach another device: no remote copies, remote signals or barrier semaphores. Data moves between devices by JAX's collectives and lax.ppermute only.
A program may use at most 64 MiB of HBM per device.

v0:
```python
import jax
import jax.numpy as jnp
from jax import lax
from jax.sharding import PartitionSpec as P

LIST = 3
xc_scale = 0.98474502
soft_square = 0.01


def exchange_potential(grid_rho):
    return -xc_scale * jnp.power(grid_rho * grid_rho + soft_square, 1.0 / 6.0)


def evaluate(points, centers, exponents, angular):
    distance = jnp.zeros(points.shape[:-2] + (points.shape[-1], centers.shape[-1]), jnp.float32)
    angular_part = jnp.ones_like(distance)
    for component in range(3):
        delta = points[..., component, :, None] - centers[..., component, None, :]
        distance = distance + delta * delta
        angular_part = angular_part + angular[..., component, None, :] * delta
    return (jnp.exp(-exponents[..., None, :] * distance) * angular_part).astype(jnp.bfloat16)


def on_device(
    points,
    centers,
    exponents,
    angular,
    grid_weights,
    hartree,
    load_plan,
    density_blocks,
    pair_lists,
    batch_pairs,
):
    slot_count = points.shape[0]
    grid_size = points.shape[3]
    columns = lax.axis_size("blk")
    per_owner = pair_lists.shape[3]
    held_pairs = density_blocks.shape[0]
    block_size = density_blocks.shape[1]
    entries = columns * per_owner
    list_size = LIST
    basis_width = list_size * block_size
    batch_rank = lax.axis_index("batch")
    plan_rows = lax.dynamic_slice_in_dim(load_plan[0], batch_rank * slot_count, slot_count)
    stored = lax.all_gather(hartree[:, 0, :], "batch", axis=0, tiled=True)
    potential = stored[plan_rows]
    wanted = pair_lists[0, 0]
    asked_slots = lax.all_to_all(wanted, "blk", split_axis=0, concat_axis=0, tiled=True)
    owner_base = jnp.arange(entries, dtype=jnp.int32) // per_owner * held_pairs
    global_ids = owner_base + wanted.reshape(entries)
    blank_table = jnp.zeros((entries, block_size, block_size), jnp.bfloat16)
    piece = lax.all_gather(density_blocks, "blk", axis=0, tiled=True)
    inside = (global_ids >= 0) & (global_ids < piece.shape[0])
    chosen = piece[jnp.clip(global_ids, 0, piece.shape[0] - 1)]
    fetched = jnp.where(inside[:, None, None], chosen, blank_table)
    group_size = 4
    loop_turns = slot_count // group_size

    def take_rows(value, turn_index):
        return lax.dynamic_slice_in_dim(value, turn_index * group_size, group_size, 0)

    def integrate(partial_table, turn_index):
        basis = evaluate(
            take_rows(points, turn_index)[:, 0],
            take_rows(centers, turn_index)[:, 0],
            take_rows(exponents, turn_index)[:, 0],
            take_rows(angular, turn_index)[:, 0],
        )
        slot_refs = take_rows(batch_pairs, turn_index)[:, 0]
        blocks = fetched[slot_refs]
        sub_density = (
            blocks.reshape(group_size, list_size, list_size, block_size, block_size)
            .transpose(0, 1, 3, 2, 4)
            .reshape(group_size, basis_width, basis_width)
        )
        inner = jnp.einsum("gpm,gmn->gpn", basis, sub_density, preferred_element_type=jnp.float32)
        grid_rho = jnp.sum(inner * basis.astype(jnp.float32), axis=-1)
        effective = take_rows(potential, turn_index) + exchange_potential(grid_rho)
        weight_rows = take_rows(grid_weights, turn_index)[:, 0]
        scaled = ((weight_rows * effective)[..., None] * basis.astype(jnp.float32)).astype(
            jnp.bfloat16
        )
        full_blocks = jnp.einsum("gpm,gpn->gmn", basis, scaled, preferred_element_type=jnp.float32)
        contributions = (
            full_blocks.reshape(group_size, list_size, block_size, list_size, block_size)
            .transpose(0, 1, 3, 2, 4)
            .reshape(group_size * list_size * list_size, block_size, block_size)
        )
        partial_table = partial_table.at[slot_refs.reshape(-1)].add(contributions)
        return (partial_table, grid_rho)

    zero_table = jnp.zeros((entries, block_size, block_size), jnp.float32)
    partial_table, rho_groups = lax.scan(integrate, zero_table, jnp.arange(loop_turns))
    grid_rho = rho_groups.reshape(slot_count, grid_size)
    received = lax.all_to_all(
        partial_table.reshape(columns, per_owner, block_size, block_size),
        "blk",
        split_axis=0,
        concat_axis=0,
        tiled=True,
    )
    owned_sums = (
        jnp.zeros((held_pairs, block_size, block_size), jnp.float32)
        .at[asked_slots.reshape(entries)]
        .add(received.reshape(entries, block_size, block_size))
    )
    hamiltonian = lax.psum(owned_sums, "batch")
    batch_total = load_plan.shape[1]
    placement = (plan_rows[None, :] == jnp.arange(batch_total, dtype=jnp.int32)[:, None]).astype(
        jnp.float32
    )
    spread_rows = jnp.dot(
        placement, grid_rho, precision=lax.Precision.HIGHEST, preferred_element_type=jnp.float32
    )
    density = lax.psum_scatter(spread_rows, "batch", scatter_dimension=0, tiled=True)
    return (hamiltonian, density[:, None, :])


def solution(mesh):
    return jax.shard_map(
        on_device,
        mesh=mesh,
        in_specs=(
            P("batch", "blk", None, None),
            P("batch", "blk", None, None),
            P("batch", "blk", None),
            P("batch", "blk", None, None),
            P("batch", "blk", None),
            P("batch", "blk", None),
            P("blk", None),
            P("blk", None, None),
            P("batch", "blk", None, None),
            P("batch", "blk", None),
        ),
        out_specs=(P("blk", None, None), P("batch", "blk", None)),
        check_vma=False,
    )
```

profile of v0, /device:TPU:8, one launch (start us, length us, event | category | flops | bytes accessed | tf_op | source)
XLA Modules:
  0.0 800.7 jit_solution(2311108223574678586)
XLA Ops:
  10.7 9.1 %all-to-all-start = ((s32[16,1,2]{2,1,0:T(1,128)}), s32[16,1,2]{2,1,0:T(1,128)S(1)}, u32[]{:S(2)}, u32[]{:S(2)}) async-start(s32[16,1,2]{2,1,0:T(1,128)} %copy.56), calls=%async_computation | async-start | bytes 16384 | tf_op jit(solution)/shard_map/all_to_all | solution.py:51
  22.3 76.3 %all-gather.6.cloned.1.call-done = f32[1024,1,256]{2,0,1:T(8,128)} async-done(((f32[32,1,256]{2,0,1:T(8,128)}), f32[1024,1,256]{2,0,1:T(8,128)}) %all-gather.6.cloned.1.call-update) | async-done | bytes 1048592 | tf_op jit(solution)/shard_map/all_gather | solution.py:48
  100.4 54.4 %all-gather.4.cloned.1.call-done = bf16[256,128,128]{2,1,0:T(8,128)(2,1)} async-done(((bf16[16,128,128]{2,1,0:T(8,128)(2,1)}), bf16[256,128,128]{2,1,0:T(8,128)(2,1)}) %all-gather.4.cloned.1.call-update) | async-done | bytes 8388624 | tf_op jit(solution)/shard_map/all_gather | solution.py:55
  154.8 4.1 gather_fusion.2
  160.6 234.9 %while.12 = (s32[]{:T(128)}, f32[32,128,128]{2,1,0:T(8,128)}, f32[8,4,256]{2,1,0:T(4,128)S(1)}, s32[8]{0:T(128)S(1)}, s32[32,1,9]{2,0,1:T(8,128)S(1)}, /*index=5...) while((s32[]{:T(128)}, f32[32,128,128]{2,1,0:T(8,128)}, ...), condition=%wide.region_3.4_spmd, body=%wide.region_0.3_spmd.sunk | while | flops 633674496 | bytes 35997664 | solution.py:96
  170.8 4.2 fusion.51
  175.1 3.5 reshape.302
  180.3 9.6 %scatter_fusion = f32[32,128,128]{2,1,0:T(8,128)} fusion(f32[32,128,128]{2,1,0:T(8,128)} %get-tuple-element.276, s32[36]{0:T(128)S(1)} %fusion.47, f32[36,128,128]{2,1,0:T(8,128)} %bitcast.106), kind=kCustom, calls=%fused_computation.3.clone.1 | custom fusion | flops 589824 | bytes 7078032 | tf_op jit(solution)/shard_map/while/body/eval_jaxpr/scatter-add | solution.py:92
  200.2 4.2 fusion.51
  204.4 3.5 reshape.302
  209.7 9.7 %scatter_fusion = f32[32,128,128]{2,1,0:T(8,128)} fusion(f32[32,128,128]{2,1,0:T(8,128)} %get-tuple-element.276, s32[36]{0:T(128)S(1)} %fusion.47, f32[36,128,128]{2,1,0:T(8,128)} %bitcast.106), kind=kCustom, calls=%fused_computation.3.clone.1 | custom fusion | flops 589824 | bytes 7078032 | tf_op jit(solution)/shard_map/while/body/eval_jaxpr/scatter-add | solution.py:92
  229.6 4.2 fusion.51
  233.8 3.5 reshape.302
  239.1 9.7 %scatter_fusion = f32[32,128,128]{2,1,0:T(8,128)} fusion(f32[32,128,128]{2,1,0:T(8,128)} %get-tuple-element.276, s32[36]{0:T(128)S(1)} %fusion.47, f32[36,128,128]{2,1,0:T(8,128)} %bitcast.106), kind=kCustom, calls=%fused_computation.3.clone.1 | custom fusion | flops 589824 | bytes 7078032 | tf_op jit(solution)/shard_map/while/body/eval_jaxpr/scatter-add | solution.py:92
  259.0 4.2 fusion.51
  263.2 3.5 reshape.302
  268.5 9.7 %scatter_fusion = f32[32,128,128]{2,1,0:T(8,128)} fusion(f32[32,128,128]{2,1,0:T(8,128)} %get-tuple-element.276, s32[36]{0:T(128)S(1)} %fusion.47, f32[36,128,128]{2,1,0:T(8,128)} %bitcast.106), kind=kCustom, calls=%fused_computation.3.clone.1 | custom fusion | flops 589824 | bytes 7078032 | tf_op jit(solution)/shard_map/while/body/eval_jaxpr/scatter-add | solution.py:92
  288.4 4.2 fusion.51
  292.6 3.5 reshape.302
  297.9 9.7 %scatter_fusion = f32[32,128,128]{2,1,0:T(8,128)} fusion(f32[32,128,128]{2,1,0:T(8,128)} %get-tuple-element.276, s32[36]{0:T(128)S(1)} %fusion.47, f32[36,128,128]{2,1,0:T(8,128)} %bitcast.106), kind=kCustom, calls=%fused_computation.3.clone.1 | custom fusion | flops 589824 | bytes 7078032 | tf_op jit(solution)/shard_map/while/body/eval_jaxpr/scatter-add | solution.py:92
  317.8 4.2 fusion.51
  322.0 3.5 reshape.302
  327.3 9.6 %scatter_fusion = f32[32,128,128]{2,1,0:T(8,128)} fusion(f32[32,128,128]{2,1,0:T(8,128)} %get-tuple-element.276, s32[36]{0:T(128)S(1)} %fusion.47, f32[36,128,128]{2,1,0:T(8,128)} %bitcast.106), kind=kCustom, calls=%fused_computation.3.clone.1 | custom fusion | flops 589824 | bytes 7078032 | tf_op jit(solution)/shard_map/while/body/eval_jaxpr/scatter-add | solution.py:92
  347.1 4.2 fusion.51
  356.6 9.6 %scatter_fusion = f32[32,128,128]{2,1,0:T(8,128)} fusion(f32[32,128,128]{2,1,0:T(8,128)} %get-tuple-element.276, s32[36]{0:T(128)S(1)} %fusion.47, f32[36,128,128]{2,1,0:T(8,128)} %bitcast.106), kind=kCustom, calls=%fused_computation.3.clone.1 | custom fusion | flops 589824 | bytes 7078032 | tf_op jit(solution)/shard_map/while/body/eval_jaxpr/scatter-add | solution.py:92
  376.5 4.2 fusion.51
  380.7 3.5 reshape.302
  386.0 9.6 %scatter_fusion = f32[32,128,128]{2,1,0:T(8,128)} fusion(f32[32,128,128]{2,1,0:T(8,128)} %get-tuple-element.276, s32[36]{0:T(128)S(1)} %fusion.47, f32[36,128,128]{2,1,0:T(8,128)} %bitcast.106), kind=kCustom, calls=%fused_computation.3.clone.1 | custom fusion | flops 589824 | bytes 7078032 | tf_op jit(solution)/shard_map/while/body/eval_jaxpr/scatter-add | solution.py:92
  395.5 6.8 all-to-all-start.1
  406.1 43.7 %all-to-all-done.1 = f32[16,2,128,128]{3,2,1,0:T(8,128)S(1)} async-done(((f32[16,2,128,128]{3,2,1,0:T(8,128)}), f32[16,2,128,128]{3,2,1,0:T(8,128)S(1)}, u32[]{:S(2)}, u32[]{:S(2)}) %all-to-all-start.1) | async-done | bytes 2097184 | tf_op jit(solution)/shard_map/all_to_all | solution.py:98
  453.5 175.6 %reduce-scatter.2.cloned.1.call-done = f32[32,256]{1,0:T(8,128)} async-done(((f32[1024,256]{1,0:T(8,128)}), f32[32,256]{1,0:T(8,128)}) %reduce-scatter.2.cloned.1.call-update) | async-done | bytes 32784 | tf_op jit(solution)/shard_map/reduce_scatter | solution.py:118
  630.5 161.3 %all-reduce.2.cloned.1.call-done = f32[16,128,128]{2,1,0:T(8,128)} async-done(((f32[16,128,128]{2,1,0:T(8,128)}), f32[16,128,128]{2,1,0:T(8,128)}) %all-reduce.2.cloned.1.call-update) | async-done | bytes 1048592 | tf_op jit(solution)/shard_map/psum | solution.py:110
  (263 shorter events, 114.2 us)
Async XLA Ops:
  7.2 91.4 %all-gather.6.cloned.1.call-start = ((), (), s32[]{:S(2)}) async-start(), calls=%async_computation.6 | async-start | bytes 1081344 | tf_op jit(solution)/shard_map/all_gather | solution.py:48
  8.6 146.2 %all-gather.4.cloned.1.call-start = ((), (), s32[]{:S(2)}) async-start(), calls=%async_computation.3 | async-start | bytes 8912896 | tf_op jit(solution)/shard_map/all_gather | solution.py:55
  10.7 384.8 %all-to-all-start = ((s32[16,1,2]{2,1,0:T(1,128)}), s32[16,1,2]{2,1,0:T(1,128)S(1)}, u32[]{:S(2)}, u32[]{:S(2)}) async-start(s32[16,1,2]{2,1,0:T(1,128)} %copy.56), calls=%async_computation | async-start | bytes 16384 | tf_op jit(solution)/shard_map/all_to_all | solution.py:51
  160.6 3.8 copy-start
  180.3 9.6 %copy-start.1 = (bf16[32,128,128]{2,1,0:T(8,128)(2,1)S(1)}, bf16[32,128,128]{2,1,0:T(8,128)(2,1)}, u32[]{:S(2)}) copy-start(bf16[32,128,128]{2,1,0:T(8,128)(2,1)} %copy-done) | copy-start | bytes 3145732 | tf_op jit(solution)/shard_map/while
  190.0 3.8 copy-start
  209.7 9.7 %copy-start.1 = (bf16[32,128,128]{2,1,0:T(8,128)(2,1)S(1)}, bf16[32,128,128]{2,1,0:T(8,128)(2,1)}, u32[]{:S(2)}) copy-start(bf16[32,128,128]{2,1,0:T(8,128)(2,1)} %copy-done) | copy-start | bytes 3145732 | tf_op jit(solution)/shard_map/while
  219.4 3.8 copy-start
  239.1 9.7 %copy-start.1 = (bf16[32,128,128]{2,1,0:T(8,128)(2,1)S(1)}, bf16[32,128,128]{2,1,0:T(8,128)(2,1)}, u32[]{:S(2)}) copy-start(bf16[32,128,128]{2,1,0:T(8,128)(2,1)} %copy-done) | copy-start | bytes 3145732 | tf_op jit(solution)/shard_map/while
  248.8 3.8 copy-start
  268.5 9.8 %copy-start.1 = (bf16[32,128,128]{2,1,0:T(8,128)(2,1)S(1)}, bf16[32,128,128]{2,1,0:T(8,128)(2,1)}, u32[]{:S(2)}) copy-start(bf16[32,128,128]{2,1,0:T(8,128)(2,1)} %copy-done) | copy-start | bytes 3145732 | tf_op jit(solution)/shard_map/while
  278.2 3.8 copy-start
  297.9 9.7 %copy-start.1 = (bf16[32,128,128]{2,1,0:T(8,128)(2,1)S(1)}, bf16[32,128,128]{2,1,0:T(8,128)(2,1)}, u32[]{:S(2)}) copy-start(bf16[32,128,128]{2,1,0:T(8,128)(2,1)} %copy-done) | copy-start | bytes 3145732 | tf_op jit(solution)/shard_map/while
  307.6 3.8 copy-start
  327.3 9.6 %copy-start.1 = (bf16[32,128,128]{2,1,0:T(8,128)(2,1)S(1)}, bf16[32,128,128]{2,1,0:T(8,128)(2,1)}, u32[]{:S(2)}) copy-start(bf16[32,128,128]{2,1,0:T(8,128)(2,1)} %copy-done) | copy-start | bytes 3145732 | tf_op jit(solution)/shard_map/while
  336.9 3.8 copy-start
  356.6 9.6 %copy-start.1 = (bf16[32,128,128]{2,1,0:T(8,128)(2,1)S(1)}, bf16[32,128,128]{2,1,0:T(8,128)(2,1)}, u32[]{:S(2)}) copy-start(bf16[32,128,128]{2,1,0:T(8,128)(2,1)} %copy-done) | copy-start | bytes 3145732 | tf_op jit(solution)/shard_map/while
  366.3 3.8 copy-start
  386.0 9.6 %copy-start.1 = (bf16[32,128,128]{2,1,0:T(8,128)(2,1)S(1)}, bf16[32,128,128]{2,1,0:T(8,128)(2,1)}, u32[]{:S(2)}) copy-start(bf16[32,128,128]{2,1,0:T(8,128)(2,1)} %copy-done) | copy-start | bytes 3145732 | tf_op jit(solution)/shard_map/while
  395.5 54.2 %all-to-all-start.1 = ((f32[16,2,128,128]{3,2,1,0:T(8,128)}), f32[16,2,128,128]{3,2,1,0:T(8,128)S(1)}, u32[]{:S(2)}, u32[]{:S(2)}) async-start(f32[16,2,128,128]{3,2,1,0:T(8,128)} %bitcast.108), calls=%async_computation.1 | async-start | bytes 4194304 | tf_op jit(solution)/shard_map/all_to_all | solution.py:98
  402.4 226.8 %reduce-scatter.2.cloned.1.call-start = ((), (), s32[]{:S(2)}) async-start(), calls=%async_computation.5 | async-start | bytes 1081344 | tf_op jit(solution)/shard_map/reduce_scatter | solution.py:118
  404.7 387.1 %all-reduce.2.cloned.1.call-start = ((), (), s32[]{:S(2)}) async-start(), calls=%async_computation.4 | async-start | bytes 2097152 | tf_op jit(solution)/shard_map/psum | solution.py:110
  452.5 1.0 copy-start.2
Sparse Core Ops, SparseCore 0:
  11.7 86.7 all-gather.5
  100.7 54.0 all-gather.3
  407.6 221.4 reduce-scatter.1
  633.0 158.7 all-reduce.1
where the time goes:
time: 804 us; the launch traced here: 801 us
  waiting for transfers between devices  512 us (64%)
  local copies, waits for them, and re-layouts  112 us (14%)
  other arithmetic  81.9 us (10%)
  matrix products  58.4 us (7%)
  starting transfers between devices  16.1 us (2%)
  between operations  13.9 us (2%)
    reduce_scatter x1, waiting for transfers between devices, on_device(): lax.psum_scatter(spread_rows, 'batch', scatter_dimension=0, tiled=True)  176 us
    psum x1, waiting for transfers between devices, on_device(): hamiltonian = lax.psum(owned_sums, 'batch')  161 us
    scatter-add x8, other arithmetic, integrate(): partial_table = partial_table.at[slot_refs.reshape(-1)].add(contributions)  77.2 us
    all_gather x1, waiting for transfers between devices, on_device(): stored = lax.all_gather(hartree[:, 0, :], 'batch', axis=0, tiled=True)  76.3 us
    all_gather x1, waiting for transfers between devices, on_device(): piece = lax.all_gather(density_blocks, 'blk', axis=0, tiled=True)  54.4 us
    all_to_all x1, waiting for transfers between devices, on_device(): lax.all_to_all(partial_table.reshape(columns, per_owner, block_size, bloc...  43.7 us
    dot_general x8, matrix products, integrate(): jnp.einsum('gpm,gpn->gmn', basis, scaled, preferred_element_type=jnp.floa...  33.7 us
    reshape x8, local copies, waits for them, and re-layouts, integrate(): full_blocks.reshape(group_size, list_size, block_size, list_size, block_s...  27.7 us
  transfers between devices with their start and end apart: 6, of which 5 were waited for; matrix products, arithmetic and copies ran while one was open for 31% of the time, Pallas kernels for 0%

commit v1 on v0

--- a/solution.py
+++ b/solution.py
@@ -52,7 +52,9 @@
     owner_base = jnp.arange(entries, dtype=jnp.int32) // per_owner * held_pairs
     global_ids = owner_base + wanted.reshape(entries)
     blank_table = jnp.zeros((entries, block_size, block_size), jnp.bfloat16)
-    piece = lax.all_gather(density_blocks, "blk", axis=0, tiled=True)
+    piece = jnp.concatenate(
+        lax.all_to_all(jnp.stack([density_blocks] * lax.axis_size("blk")), "blk", 0, 0), axis=0
+    )
     inside = (global_ids >= 0) & (global_ids < piece.shape[0])
     chosen = piece[jnp.clip(global_ids, 0, piece.shape[0] - 1)]
     fetched = jnp.where(inside[:, None, None], chosen, blank_table)

time: 804 us -> 864 us (1.075)
  waiting for transfers between devices: 512 us -> 560 us
    all_to_all x0 -> x1, waiting for transfers between devices: none -> 92.4 us  [on_device(): lax.all_to_all(jnp.stack([density_blocks] * lax.axis_size('blk')), 'blk',...]
    all_gather x1 -> x0, waiting for transfers between devices: 54.4 us -> none  [on_device(): piece = lax.all_gather(density_blocks, 'blk', axis=0, tiled=True)]
    all_to_all x0 -> x1, starting transfers between devices: none -> 10.4 us  [on_device(): lax.all_to_all(jnp.stack([density_blocks] * lax.axis_size('blk')), 'blk',...]
    all_gather x1, waiting for transfers between devices: 76.3 us -> 85.8 us  [on_device(): stored = lax.all_gather(hartree[:, 0, :], 'batch', axis=0, tiled=True)]
  transfers between devices with their start and end apart: 6 -> 6, of which waited for: 5 -> 5; matrix products, arithmetic and copies ran while one was open for 31% -> 29% of each run, Pallas kernels for 0% -> 0%
where the time goes in v1:
time: 864 us; the launch traced here: 860 us
  waiting for transfers between devices  560 us (65%)
  local copies, waits for them, and re-layouts  116 us (13%)
  other arithmetic  81.9 us (9%)
  matrix products  58.3 us (7%)
  starting transfers between devices  24.3 us (3%)
  between operations  13.9 us (2%)
    reduce_scatter x1, waiting for transfers between devices, on_device(): lax.psum_scatter(spread_rows, 'batch', scatter_dimension=0, tiled=True)  176 us
    psum x1, waiting for transfers between devices, on_device(): hamiltonian = lax.psum(owned_sums, 'batch')  161 us
    all_to_all x1, waiting for transfers between devices, on_device(): lax.all_to_all(jnp.stack([density_blocks] * lax.axis_size('blk')), 'blk',...  92.4 us
    all_gather x1, waiting for transfers between devices, on_device(): stored = lax.all_gather(hartree[:, 0, :], 'batch', axis=0, tiled=True)  85.8 us
    scatter-add x8, other arithmetic, integrate(): partial_table = partial_table.at[slot_refs.reshape(-1)].add(contributions)  77.3 us
    all_to_all x1, waiting for transfers between devices, on_device(): lax.all_to_all(partial_table.reshape(columns, per_owner, block_size, bloc...  43.7 us
    dot_general x8, matrix products, integrate(): jnp.einsum('gpm,gpn->gmn', basis, scaled, preferred_element_type=jnp.floa...  33.6 us
    reshape x8, local copies, waits for them, and re-layouts, integrate(): full_blocks.reshape(group_size, list_size, block_size, list_size, block_s...  27.7 us
  transfers between devices with their start and end apart: 6, of which 5 were waited for; matrix products, arithmetic and copies ran while one was open for 29% of the time, Pallas kernels for 0%

profile of v1, /device:TPU:8, one launch (start us, length us, event | category | flops | bytes accessed | tf_op | source)
XLA Modules:
  0.0 860.0 jit_solution(5259896202348821484)
XLA Ops:
  7.2 6.4 stack.2
  13.6 10.4 %all-to-all-start.1 = ((bf16[16,16,128,128]{3,2,1,0:T(8,128)(2,1)}), bf16[16,16,128,128]{3,2,1,0:T(8,128)(2,1)}, u32[]{:S(2)}, u32[]{:S(2)}) async-start(bf16[16,16,128,128]{3,2,1,0:T(8,128)(2,1)} %stack.2), calls=%async_computation.1 | async-start | bytes 16777216 | tf_op jit(solution)/shard_map/all_to_all | solution.py:56
  26.6 85.8 %all-gather.3.cloned.1.call-done = f32[1024,1,256]{2,0,1:T(8,128)} async-done(((f32[32,1,256]{2,0,1:T(8,128)}), f32[1024,1,256]{2,0,1:T(8,128)}) %all-gather.3.cloned.1.call-update) | async-done | bytes 1048592 | tf_op jit(solution)/shard_map/all_gather | solution.py:48
  114.2 92.4 %all-to-all-done.1 = bf16[16,16,128,128]{3,2,1,0:T(8,128)(2,1)} async-done(((bf16[16,16,128,128]{3,2,1,0:T(8,128)(2,1)}), bf16[16,16,128,128]{3,2,1,0:T(8,128)(2,1)}, u32[]{:S(2)}, u32[]{:S(2)}) %all-to-all-start.1) | async-done | bytes 8388640 | tf_op jit(solution)/shard_map/all_to_all | solution.py:56
  206.7 6.4 all-to-all-start
  213.1 4.1 gather_fusion.2
  218.9 234.9 %while.12 = (s32[]{:T(128)}, f32[32,128,128]{2,1,0:T(8,128)}, f32[8,4,256]{2,1,0:T(4,128)S(1)}, s32[8]{0:T(128)S(1)}, s32[32,1,9]{2,0,1:T(8,128)S(1)}, /*index=5...) while((s32[]{:T(128)}, f32[32,128,128]{2,1,0:T(8,128)}, ...), condition=%wide.region_3.4_spmd, body=%wide.region_0.3_spmd.sunk | while | flops 633674496 | bytes 35997664 | solution.py:98
  229.1 4.2 fusion.51
  233.3 3.5 reshape.308
  238.6 9.6 %scatter_fusion = f32[32,128,128]{2,1,0:T(8,128)} fusion(f32[32,128,128]{2,1,0:T(8,128)} %get-tuple-element.276, s32[36]{0:T(128)S(1)} %fusion.47, f32[36,128,128]{2,1,0:T(8,128)} %bitcast.107), kind=kCustom, calls=%fused_computation.3.clone.1 | custom fusion | flops 589824 | bytes 7078032 | tf_op jit(solution)/shard_map/while/body/eval_jaxpr/scatter-add | solution.py:94
  258.4 4.2 fusion.51
  262.7 3.5 reshape.308
  267.9 9.7 %scatter_fusion = f32[32,128,128]{2,1,0:T(8,128)} fusion(f32[32,128,128]{2,1,0:T(8,128)} %get-tuple-element.276, s32[36]{0:T(128)S(1)} %fusion.47, f32[36,128,128]{2,1,0:T(8,128)} %bitcast.107), kind=kCustom, calls=%fused_computation.3.clone.1 | custom fusion | flops 589824 | bytes 7078032 | tf_op jit(solution)/shard_map/while/body/eval_jaxpr/scatter-add | solution.py:94
  287.9 4.2 fusion.51
  292.1 3.5 reshape.308
  297.3 9.7 %scatter_fusion = f32[32,128,128]{2,1,0:T(8,128)} fusion(f32[32,128,128]{2,1,0:T(8,128)} %get-tuple-element.276, s32[36]{0:T(128)S(1)} %fusion.47, f32[36,128,128]{2,1,0:T(8,128)} %bitcast.107), kind=kCustom, calls=%fused_computation.3.clone.1 | custom fusion | flops 589824 | bytes 7078032 | tf_op jit(solution)/shard_map/while/body/eval_jaxpr/scatter-add | solution.py:94
  317.3 4.2 fusion.51
  326.8 9.7 %scatter_fusion = f32[32,128,128]{2,1,0:T(8,128)} fusion(f32[32,128,128]{2,1,0:T(8,128)} %get-tuple-element.276, s32[36]{0:T(128)S(1)} %fusion.47, f32[36,128,128]{2,1,0:T(8,128)} %bitcast.107), kind=kCustom, calls=%fused_computation.3.clone.1 | custom fusion | flops 589824 | bytes 7078032 | tf_op jit(solution)/shard_map/while/body/eval_jaxpr/scatter-add | solution.py:94
  346.7 4.2 fusion.51
  356.2 9.7 %scatter_fusion = f32[32,128,128]{2,1,0:T(8,128)} fusion(f32[32,128,128]{2,1,0:T(8,128)} %get-tuple-element.276, s32[36]{0:T(128)S(1)} %fusion.47, f32[36,128,128]{2,1,0:T(8,128)} %bitcast.107), kind=kCustom, calls=%fused_computation.3.clone.1 | custom fusion | flops 589824 | bytes 7078032 | tf_op jit(solution)/shard_map/while/body/eval_jaxpr/scatter-add | solution.py:94
  376.0 4.2 fusion.51
  380.2 3.5 reshape.308
  385.5 9.6 %scatter_fusion = f32[32,128,128]{2,1,0:T(8,128)} fusion(f32[32,128,128]{2,1,0:T(8,128)} %get-tuple-element.276, s32[36]{0:T(128)S(1)} %fusion.47, f32[36,128,128]{2,1,0:T(8,128)} %bitcast.107), kind=kCustom, calls=%fused_computation.3.clone.1 | custom fusion | flops 589824 | bytes 7078032 | tf_op jit(solution)/shard_map/while/body/eval_jaxpr/scatter-add | solution.py:94
  405.4 4.2 fusion.51
  409.6 3.5 reshape.308
  414.9 9.6 %scatter_fusion = f32[32,128,128]{2,1,0:T(8,128)} fusion(f32[32,128,128]{2,1,0:T(8,128)} %get-tuple-element.276, s32[36]{0:T(128)S(1)} %fusion.47, f32[36,128,128]{2,1,0:T(8,128)} %bitcast.107), kind=kCustom, calls=%fused_computation.3.clone.1 | custom fusion | flops 589824 | bytes 7078032 | tf_op jit(solution)/shard_map/while/body/eval_jaxpr/scatter-add | solution.py:94
  434.7 4.2 fusion.51
  444.2 9.6 %scatter_fusion = f32[32,128,128]{2,1,0:T(8,128)} fusion(f32[32,128,128]{2,1,0:T(8,128)} %get-tuple-element.276, s32[36]{0:T(128)S(1)} %fusion.47, f32[36,128,128]{2,1,0:T(8,128)} %bitcast.107), kind=kCustom, calls=%fused_computation.3.clone.1 | custom fusion | flops 589824 | bytes 7078032 | tf_op jit(solution)/shard_map/while/body/eval_jaxpr/scatter-add | solution.py:94
  453.8 7.3 all-to-all-start.2
  464.8 43.7 %all-to-all-done.2 = f32[16,2,128,128]{3,2,1,0:T(8,128)S(1)} async-done(((f32[16,2,128,128]{3,2,1,0:T(8,128)}), f32[16,2,128,128]{3,2,1,0:T(8,128)S(1)}, u32[]{:S(2)}, u32[]{:S(2)}) %all-to-all-start.2) | async-done | bytes 2097184 | tf_op jit(solution)/shard_map/all_to_all | solution.py:100
  512.3 176.1 %reduce-scatter.2.cloned.1.call-done = f32[32,256]{1,0:T(8,128)} async-done(((f32[1024,256]{1,0:T(8,128)}), f32[32,256]{1,0:T(8,128)}) %reduce-scatter.2.cloned.1.call-update) | async-done | bytes 32784 | tf_op jit(solution)/shard_map/reduce_scatter | solution.py:120
  689.8 161.4 %all-reduce.2.cloned.1.call-done = f32[16,128,128]{2,1,0:T(8,128)} async-done(((f32[16,128,128]{2,1,0:T(8,128)}), f32[16,128,128]{2,1,0:T(8,128)}) %all-reduce.2.cloned.1.call-update) | async-done | bytes 1048592 | tf_op jit(solution)/shard_map/psum | solution.py:112
  (269 shorter events, 117.7 us)
Async XLA Ops:
  13.6 10.5 %copy-start.3 = (f32[32,1,256]{2,1,0:T(1,128)S(1)}, f32[32,1,256]{2,1,0:T(1,128)}, u32[]{:S(2)}) copy-start(f32[32,1,256]{2,1,0:T(1,128)} %param.17) | copy-start | bytes 98308
  13.6 11.2 %copy-start.5 = (s32[1,1,16,2]{2,3,1,0:T(2,128)S(1)}, s32[1,1,16,2]{2,3,1,0:T(2,128)}, u32[]{:S(2)}) copy-start(s32[1,1,16,2]{2,3,1,0:T(2,128)} %param.20) | copy-start | bytes 388
  13.6 11.5 %copy-start.4 = (s32[32,1,9]{0,1,2:T(1,128)S(1)}, s32[32,1,9]{0,1,2:T(1,128)}, u32[]{:S(2)}) copy-start(s32[32,1,9]{0,1,2:T(1,128)} %param.21) | copy-start | bytes 3460
  13.6 193.1 %all-to-all-start.1 = ((bf16[16,16,128,128]{3,2,1,0:T(8,128)(2,1)}), bf16[16,16,128,128]{3,2,1,0:T(8,128)(2,1)}, u32[]{:S(2)}, u32[]{:S(2)}) async-start(bf16[16,16,128,128]{3,2,1,0:T(8,128)(2,1)} %stack.2), calls=%async_computation.1 | async-start | bytes 16777216 | tf_op jit(solution)/shard_map/all_to_all | solution.py:56
  24.0 88.4 %all-gather.3.cloned.1.call-start = ((), (), s32[]{:S(2)}) async-start(), calls=%async_computation.6 | async-start | bytes 1081344 | tf_op jit(solution)/shard_map/all_gather | solution.py:48
  206.7 247.2 %all-to-all-start = ((s32[16,1,2]{2,1,0:T(1,128)}), s32[16,1,2]{2,1,0:T(1,128)S(1)}, u32[]{:S(2)}, u32[]{:S(2)}) async-start(s32[16,1,2]{2,1,0:T(1,128)} %copy.56), calls=%async_computation | async-start | bytes 16384 | tf_op jit(solution)/shard_map/all_to_all | solution.py:51
  218.9 3.8 copy-start
  238.6 9.7 %copy-start.1 = (bf16[32,128,128]{2,1,0:T(8,128)(2,1)S(1)}, bf16[32,128,128]{2,1,0:T(8,128)(2,1)}, u32[]{:S(2)}) copy-start(bf16[32,128,128]{2,1,0:T(8,128)(2,1)} %copy-done) | copy-start | bytes 3145732 | tf_op jit(solution)/shard_map/while
  248.2 3.8 copy-start
  267.9 9.7 %copy-start.1 = (bf16[32,128,128]{2,1,0:T(8,128)(2,1)S(1)}, bf16[32,128,128]{2,1,0:T(8,128)(2,1)}, u32[]{:S(2)}) copy-start(bf16[32,128,128]{2,1,0:T(8,128)(2,1)} %copy-done) | copy-start | bytes 3145732 | tf_op jit(solution)/shard_map/while
  277.6 3.8 copy-start
  297.3 9.7 %copy-start.1 = (bf16[32,128,128]{2,1,0:T(8,128)(2,1)S(1)}, bf16[32,128,128]{2,1,0:T(8,128)(2,1)}, u32[]{:S(2)}) copy-start(bf16[32,128,128]{2,1,0:T(8,128)(2,1)} %copy-done) | copy-start | bytes 3145732 | tf_op jit(solution)/shard_map/while
  307.1 3.8 copy-start
  326.8 9.7 %copy-start.1 = (bf16[32,128,128]{2,1,0:T(8,128)(2,1)S(1)}, bf16[32,128,128]{2,1,0:T(8,128)(2,1)}, u32[]{:S(2)}) copy-start(bf16[32,128,128]{2,1,0:T(8,128)(2,1)} %copy-done) | copy-start | bytes 3145732 | tf_op jit(solution)/shard_map/while
  336.5 3.8 copy-start
  356.2 9.7 %copy-start.1 = (bf16[32,128,128]{2,1,0:T(8,128)(2,1)S(1)}, bf16[32,128,128]{2,1,0:T(8,128)(2,1)}, u32[]{:S(2)}) copy-start(bf16[32,128,128]{2,1,0:T(8,128)(2,1)} %copy-done) | copy-start | bytes 3145732 | tf_op jit(solution)/shard_map/while
  365.8 3.8 copy-start
  385.5 9.6 %copy-start.1 = (bf16[32,128,128]{2,1,0:T(8,128)(2,1)S(1)}, bf16[32,128,128]{2,1,0:T(8,128)(2,1)}, u32[]{:S(2)}) copy-start(bf16[32,128,128]{2,1,0:T(8,128)(2,1)} %copy-done) | copy-start | bytes 3145732 | tf_op jit(solution)/shard_map/while
  395.2 3.8 copy-start
  414.9 9.7 %copy-start.1 = (bf16[32,128,128]{2,1,0:T(8,128)(2,1)S(1)}, bf16[32,128,128]{2,1,0:T(8,128)(2,1)}, u32[]{:S(2)}) copy-start(bf16[32,128,128]{2,1,0:T(8,128)(2,1)} %copy-done) | copy-start | bytes 3145732 | tf_op jit(solution)/shard_map/while
  424.5 3.8 copy-start
  444.2 9.6 %copy-start.1 = (bf16[32,128,128]{2,1,0:T(8,128)(2,1)S(1)}, bf16[32,128,128]{2,1,0:T(8,128)(2,1)}, u32[]{:S(2)}) copy-start(bf16[32,128,128]{2,1,0:T(8,128)(2,1)} %copy-done) | copy-start | bytes 3145732 | tf_op jit(solution)/shard_map/while
  453.8 54.7 %all-to-all-start.2 = ((f32[16,2,128,128]{3,2,1,0:T(8,128)}), f32[16,2,128,128]{3,2,1,0:T(8,128)S(1)}, u32[]{:S(2)}, u32[]{:S(2)}) async-start(f32[16,2,128,128]{3,2,1,0:T(8,128)} %bitcast.109), calls=%async_computation.2 | async-start | bytes 4194304 | tf_op jit(solution)/shard_map/all_to_all | solution.py:100
  461.2 227.3 %reduce-scatter.2.cloned.1.call-start = ((), (), s32[]{:S(2)}) async-start(), calls=%async_computation.5 | async-start | bytes 1081344 | tf_op jit(solution)/shard_map/reduce_scatter | solution.py:120
  463.5 387.7 %all-reduce.2.cloned.1.call-start = ((), (), s32[]{:S(2)}) async-start(), calls=%async_computation.4 | async-start | bytes 2097152 | tf_op jit(solution)/shard_map/psum | solution.py:112
  511.3 1.0 copy-start.2
Sparse Core Ops, SparseCore 0:
  28.6 83.7 all-gather.2
  466.4 221.9 reduce-scatter.1
  692.5 158.7 all-reduce.1
